TPU v7x, 32 devices: a whole 2x2x4 slice. The times are simulated.
32 devices in a mesh: groups: 2 (over y), hosts: 8 (over z, x), tensor: 2 (over core).
Axes of the slice: x: 2, y: 2, z: 4, core: 2. Of those that a mesh axis runs over, the one named last changes fastest.
Arguments:
- context_queries: bfloat16 [2048, 8192], P(('groups', 'hosts'), 'tensor'), parts along dimension 0, may hold values from -6 to 6
- context_keys: bfloat16 [2048, 1024], P(('groups', 'hosts'), 'tensor'), parts along dimension 0, may hold values from -6 to 6
- context_values: bfloat16 [2048, 1024], P(('groups', 'hosts'), 'tensor'), parts along dimension 0, may hold values from -6 to 6
- doc_ids: int32 [2048], P(('groups', 'hosts')), parts along dimension 0, may hold values from 0 to 31, never falling along the last dimension, each value on 1 to 128 neighbouring positions
- query_token_rows: bfloat16 [16, 8192], P(('groups', 'hosts'), 'tensor'), parts along dimension 0, may hold values from -6 to 6
- span_start: int32 [16], P(('groups', 'hosts')), parts along dimension 0, may hold values from 0 to 511
Outputs:
- block_out: bfloat16 [2048, 8192], P(('groups', 'hosts'), 'tensor'), parts along dimension 0
- answer: bfloat16 [16, 8192], P(('groups', 'hosts'), 'tensor'), parts along dimension 0
There are 2 independent parts, one for each index of `groups`. A program takes and returns all parts, laid end to end along the dimension named above; each array names one. Nothing has to cross between parts.
All inputs are finite; a program needn't handle non-finite values.
Results may differ from a plain program's by a relative error of at most 0.0043.
Values may be sent and summed in bfloat16 or wider, within the bound.
A program may use at most 64 MiB of HBM per device.

v0:
```python
import jax
import jax.numpy as jnp
from jax import lax
from jax.sharding import PartitionSpec as P

HEAD_SIZE = 128
MASKED_SCORE = -1e30


def from_root(value, axis, source):
    kept = jnp.where(lax.axis_index(axis) == source, value, 0).astype(value.dtype)
    return lax.psum(kept, axis)


def head_groups(matrix, kv_count):
    count_rows = matrix.shape[0]
    return matrix.reshape(
        count_rows, kv_count, matrix.shape[1] // (kv_count * HEAD_SIZE), HEAD_SIZE
    ).transpose(1, 0, 2, 3)


def kv_groups(matrix, kv_count):
    return matrix.reshape(matrix.shape[0], kv_count, HEAD_SIZE).transpose(1, 0, 2)


def block_attention(queries, key_rows, value_rows, visible, factor):
    kv_count = key_rows.shape[1] // HEAD_SIZE

    def block_per_head(operands):
        query_part, key_part, value_part = operands
        scores = (
            jnp.einsum("rgd,sd->rgs", query_part, key_part, preferred_element_type=jnp.float32)
            * factor
        )
        shown = visible[:, None, :]
        peak_score = jnp.max(jnp.where(shown, scores, MASKED_SCORE), -1, keepdims=True)
        weights = jnp.where(shown, jnp.exp(scores - peak_score), 0.0)
        totals = jnp.sum(weights, -1)
        output = jnp.einsum(
            "rgs,sd->rgd",
            weights.astype(jnp.bfloat16),
            value_part,
            preferred_element_type=jnp.float32,
        )
        return (output / totals[..., None]).astype(jnp.bfloat16)

    outputs = lax.map(
        block_per_head,
        (
            head_groups(queries, kv_count),
            kv_groups(key_rows, kv_count),
            kv_groups(value_rows, kv_count),
        ),
    )
    return outputs.transpose(1, 0, 2, 3).reshape(queries.shape[0], queries.shape[1])


def query_partials(queries, key_rows, value_rows, visible, factor):
    kv_count = key_rows.shape[1] // HEAD_SIZE

    def query_per_head(operands):
        query_part, key_part, value_part = operands
        scores = (
            jnp.einsum("qgd,sd->qgs", query_part, key_part, preferred_element_type=jnp.float32)
            * factor
        )
        shown = visible[:, None, :]
        peak_score = jnp.max(jnp.where(shown, scores, MASKED_SCORE), -1)
        weights = jnp.where(shown, jnp.exp(scores - peak_score[..., None]), 0.0)
        totals = jnp.sum(weights, -1)
        partial_acc = jnp.einsum(
            "qgs,sd->qgd",
            weights.astype(jnp.bfloat16),
            value_part,
            preferred_element_type=jnp.float32,
        )
        return (peak_score, totals, partial_acc)

    peaks, totals, accums = lax.map(
        query_per_head,
        (
            head_groups(queries, kv_count),
            kv_groups(key_rows, kv_count),
            kv_groups(value_rows, kv_count),
        ),
    )
    query_count = queries.shape[0]
    peaks = peaks.transpose(1, 0, 2).reshape(query_count, -1)
    totals = totals.transpose(1, 0, 2).reshape(query_count, -1)
    accums = accums.transpose(1, 0, 2, 3).reshape(query_count, -1)
    return (peaks, totals, accums)


def on_device(context_queries, context_keys, context_values, doc_ids, query_token_rows, span_start):
    factor = float(HEAD_SIZE) ** (-0.5)
    host_index = lax.axis_index("hosts")
    host_count = lax.axis_size("hosts")
    block_len = context_queries.shape[0]
    per_host = query_token_rows.shape[0]
    stacked = jnp.stack([context_keys, context_values])
    anchor = from_root(stacked, "hosts", 0)
    key_rows = jnp.concatenate([anchor[0], context_keys], 0)
    value_rows = jnp.concatenate([anchor[1], context_values], 0)
    positions = jnp.arange(block_len, dtype=jnp.int32)
    causal = positions[None, :] <= positions[:, None]
    own_visible = causal & (doc_ids[:, None] == doc_ids[None, :])
    front_visible = jnp.broadcast_to(host_index > 0, (block_len, block_len))
    visible = jnp.concatenate([front_visible, own_visible], 1)
    block_out = block_attention(context_queries, key_rows, value_rows, visible, factor)
    all_queries, all_spans = (
        lax.all_gather(query_token_rows, "hosts", axis=0, tiled=True),
        lax.all_gather(span_start, "hosts", axis=0, tiled=True),
    )
    key_positions = host_index * block_len + positions
    query_visible = key_positions[None, :] >= all_spans[:, None]
    peaks, totals, accums = query_partials(
        all_queries, context_keys, context_values, query_visible, factor
    )
    received = (
        lax.all_to_all(peaks, "hosts", split_axis=0, concat_axis=0, tiled=True),
        lax.all_to_all(totals, "hosts", split_axis=0, concat_axis=0, tiled=True),
        lax.all_to_all(accums, "hosts", split_axis=0, concat_axis=0, tiled=True),
    )
    source_peaks = received[0].reshape(host_count, per_host, -1)
    source_totals = received[1].reshape(host_count, per_host, -1)
    source_accums = received[2].reshape(host_count, per_host, -1)
    overall = jnp.max(source_peaks, 0)
    scales = jnp.exp(source_peaks - overall[None])
    own_totals = jnp.sum(scales * source_totals, 0)
    own_accums = jnp.sum(jnp.repeat(scales, HEAD_SIZE, axis=2) * source_accums, 0)
    answer = (own_accums / jnp.repeat(own_totals, HEAD_SIZE, axis=1)).astype(jnp.bfloat16)
    return (block_out, answer)


def solution(mesh):
    in_specs = (
        P(("groups", "hosts"), "tensor"),
        P(("groups", "hosts"), "tensor"),
        P(("groups", "hosts"), "tensor"),
        P(("groups", "hosts")),
        P(("groups", "hosts"), "tensor"),
        P(("groups", "hosts")),
    )
    out_specs = (P(("groups", "hosts"), "tensor"), P(("groups", "hosts"), "tensor"))
    return jax.shard_map(
        on_device, mesh=mesh, in_specs=in_specs, out_specs=out_specs, check_vma=False
    )
```

profile of v0, /device:TPU:0, one launch (start us, length us, event | category | flops | bytes accessed | tf_op | source)
XLA Modules:
  0.0 166.9 jit_solution(4238791645243524496)
XLA Ops:
  7.2 1.1 copy.26
  9.0 0.6 copy-done.5
  9.6 0.6 dynamic-slice
  10.2 0.8 dynamic-update-slice
  11.1 13.1 %all-reduce.1 = s32[8]{0:T(128)S(1)} all-reduce(s32[8]{0:T(128)S(1)} %dynamic-update-slice), channel_id=1, replica_groups=mesh['groups'=2,'hosts'=8,'tensor'=2] {'hosts'}, use_global_device_ids=true, to_apply=%add.1 | all-reduce | flops 8 | bytes 64
  24.2 30.5 %all-gather = bf16[8,1,4096]{2,1,0:T(2,128)(2,1)S(1)} all-gather(bf16[1,1,4096]{2,1,0:T(2,128)(2,1)S(1)} %bitcast.124), channel_id=1, replica_groups=mesh['groups'=2,'hosts'=8,'tensor'=2] {'hosts'}, dimensions={0}, use_global_device_ids=true | all-gather | bytes 73728 | tf_op jit(solution)/shard_map/all_gather | solution.py:111
  54.7 0.4 reduce.5
  55.1 2.7 %while.26 = (s32[]{:T(128)}, f32[4,8,8]{2,1,0:T(8,128)S(1)}, f32[4,8,8]{2,1,0:T(8,128)S(1)}, f32[4,8,8,128]{3,2,1,0:T(8,128)S(1)}, bf16[4,8,8,128]{3,2,0,1:T(8,1...) while((s32[]{:T(128)}, f32[4,8,8]{2,1,0:T(8,128)S(1)}, ...), condition=%wide.region_8.9_spmd.clone, body=%wide.region_5.8_spmd.clone.sunk | while | flops 4268930 | bytes 241033 | solution.py:79
  55.1 0.2 select_reduce_fusion.3
  55.4 0.2 fusion.74
  55.8 0.2 select_reduce_fusion.3
  56.0 0.2 fusion.74
  56.2 0.2 fusion.73
  56.5 0.2 select_reduce_fusion.3
  56.7 0.2 fusion.74
  56.9 0.2 fusion.73
  57.2 0.2 select_reduce_fusion.3
  57.4 0.2 fusion.74
  57.8 0.7 all_to_all.18
  58.5 3.3 %all-to-all-start = ((f32[8,1,32]{2,1,0:T(1,128)}), f32[8,1,32]{2,1,0:T(1,128)S(1)}, u32[]{:S(2)}, u32[]{:S(2)}) async-start(f32[8,1,32]{2,1,0:T(1,128)} %bitcast.23), calls=%async_computation | async-start | bytes 8192 | tf_op jit(solution)/shard_map/all_to_all | solution.py:120
  61.8 0.7 all_to_all.22
  62.5 5.6 %all-to-all-done = f32[8,1,32]{2,1,0:T(1,128)S(1)} async-done(((f32[8,1,32]{2,1,0:T(1,128)}), f32[8,1,32]{2,1,0:T(1,128)S(1)}, u32[]{:S(2)}, u32[]{:S(2)}) %all-to-all-start) | async-done | bytes 1056 | tf_op jit(solution)/shard_map/all_to_all | solution.py:120
  68.1 3.3 %all-to-all-start.2 = ((f32[8,1,32]{2,1,0:T(1,128)}), f32[8,1,32]{2,1,0:T(1,128)S(1)}, u32[]{:S(2)}, u32[]{:S(2)}) async-start(f32[8,1,32]{2,1,0:T(1,128)} %bitcast.30), calls=%async_computation.2 | async-start | bytes 8192 | tf_op jit(solution)/shard_map/all_to_all | solution.py:121
  71.5 0.7 maximum_select_fusion
  72.3 0.7 copy.39
  72.9 4.9 %all-to-all-done.2 = f32[8,1,32]{2,1,0:T(1,128)S(1)} async-done(((f32[8,1,32]{2,1,0:T(1,128)}), f32[8,1,32]{2,1,0:T(1,128)S(1)}, u32[]{:S(2)}, u32[]{:S(2)}) %all-to-all-start.2) | async-done | bytes 1056 | tf_op jit(solution)/shard_map/all_to_all | solution.py:121
  77.8 3.5 %all-to-all-start.1 = ((f32[8,1,4096]{2,1,0:T(1,128)}), f32[8,1,4096]{2,1,0:T(1,128)S(1)}, u32[]{:S(2)}, u32[]{:S(2)}) async-start(f32[8,1,4096]{2,1,0:T(1,128)} %bitcast.27), calls=%async_computation.1 | async-start | bytes 262144 | tf_op jit(solution)/shard_map/all_to_all | solution.py:122
  81.4 0.7 copy.25
  82.2 6.7 %all-to-all-done.1 = f32[8,1,4096]{2,1,0:T(1,128)S(1)} async-done(((f32[8,1,4096]{2,1,0:T(1,128)}), f32[8,1,4096]{2,1,0:T(1,128)S(1)}, u32[]{:S(2)}, u32[]{:S(2)}) %all-to-all-start.1) | async-done | bytes 131104 | tf_op jit(solution)/shard_map/all_to_all | solution.py:122
  89.3 0.6 divide_convert_fusion
  89.9 58.0 %all-reduce.4.cloned.1.call-done = bf16[2,128,512]{1,2,0:T(8,128)(2,1)} async-done(((bf16[2,128,512]{1,2,0:T(8,128)(2,1)}), bf16[2,128,512]{1,2,0:T(8,128)(2,1)}) %all-reduce.4.cloned.1.call-update) | async-done | bytes 262160 | tf_op jit(solution)/shard_map/psum | solution.py:12
  147.9 1.0 fusion.52
  148.9 0.8 maximum_bitcast_fusion
  149.6 8.3 %while.25 = (s32[]{:T(128)}, bf16[4,128,8,128]{3,1,2,0:T(8,128)(2,1)S(1)}, pred[128,256]{1,0:T(8,128)(4,1)S(1)}, bf16[4,128,8,128]{1,3,2,0:T(8,128)(2,1)S(1)}, b...) while((s32[]{:T(128)}, bf16[4,128,8,128]{3,1,2,0:T(8,128)(2,1)S(1)}, ...), condition=%wide.region_4.5_spmd, body=%wide.region_1.4_spmd.sunk | while | flops 136840704 | bytes 4958285 | solution.py:47
  149.6 0.3 convolution_multiply_fusion.3
  150.0 0.4 fusion.69
  150.4 1.3 fusion.70
  151.7 0.3 convolution_multiply_fusion.3
  152.1 0.4 fusion.69
  152.5 1.3 fusion.70
  153.8 0.3 convolution_multiply_fusion.3
  154.2 0.4 fusion.69
  154.6 1.3 fusion.70
  155.9 0.3 convolution_multiply_fusion.3
  156.2 0.4 fusion.69
  156.7 1.3 fusion.70
  158.0 0.7 copy.33
  158.7 1.4 copy.53
  (40 shorter events, 1.4 us)
Async XLA Ops:
  7.2 3.7 %copy-start.2 = (bf16[128,512]{1,0:T(8,128)(2,1)S(1)}, bf16[128,512]{1,0:T(8,128)(2,1)}, u32[]{:S(2)}) copy-start(bf16[128,512]{1,0:T(8,128)(2,1)} %param.12) | copy-start | bytes 393220
  8.9 0.7 copy-start.5
  10.9 13.2 %copy-start.3 = (bf16[1,4096]{1,0:T(2,128)(2,1)S(1)}, bf16[1,4096]{1,0:T(2,128)(2,1)}, u32[]{:S(2)}) copy-start(bf16[1,4096]{1,0:T(2,128)(2,1)} %param.14) | copy-start | bytes 24580
  57.8 23.6 %copy-start = (bf16[128,4096]{1,0:T(8,128)(2,1)S(1)}, bf16[128,4096]{1,0:T(8,128)(2,1)}, u32[]{:S(2)}) copy-start(bf16[128,4096]{1,0:T(8,128)(2,1)} %param.10) | copy-start | bytes 3145732
  58.5 9.6 %all-to-all-start = ((f32[8,1,32]{2,1,0:T(1,128)}), f32[8,1,32]{2,1,0:T(1,128)S(1)}, u32[]{:S(2)}, u32[]{:S(2)}) async-start(f32[8,1,32]{2,1,0:T(1,128)} %bitcast.23), calls=%async_computation | async-start | bytes 8192 | tf_op jit(solution)/shard_map/all_to_all | solution.py:120
  68.1 9.6 %all-to-all-start.2 = ((f32[8,1,32]{2,1,0:T(1,128)}), f32[8,1,32]{2,1,0:T(1,128)S(1)}, u32[]{:S(2)}, u32[]{:S(2)}) async-start(f32[8,1,32]{2,1,0:T(1,128)} %bitcast.30), calls=%async_computation.2 | async-start | bytes 8192 | tf_op jit(solution)/shard_map/all_to_all | solution.py:121
  71.5 76.4 %all-reduce.4.cloned.1.call-start = ((), (), s32[]{:S(2)}) async-start(), calls=%async_computation.3 | async-start | bytes 524288 | tf_op jit(solution)/shard_map/psum | solution.py:12
  77.8 3.5 %copy-start.4 = (s32[128]{0:T(128)S(1)}, s32[128]{0:T(128)}, u32[]{:S(2)}) copy-start(s32[128]{0:T(128)} %param.13) | copy-start | bytes 1540
  77.8 11.1 %all-to-all-start.1 = ((f32[8,1,4096]{2,1,0:T(1,128)}), f32[8,1,4096]{2,1,0:T(1,128)S(1)}, u32[]{:S(2)}, u32[]{:S(2)}) async-start(f32[8,1,4096]{2,1,0:T(1,128)} %bitcast.27), calls=%async_computation.1 | async-start | bytes 262144 | tf_op jit(solution)/shard_map/all_to_all | solution.py:122
  82.1 67.5 %copy-start.1 = (bf16[4,128,8,128]{3,1,2,0:T(8,128)(2,1)S(1)}, bf16[4,128,8,128]{3,1,2,0:T(8,128)(2,1)}, u32[]{:S(2)}) copy-start(bf16[4,128,8,128]{3,1,2,0:T(8,128)(2,1)} %custom-call) | copy-start | bytes 3145732
Sparse Core Ops, SparseCore 0:
  75.7 72.1 all-reduce.3
where the time goes:
time: 168 us; the launch traced here: 167 us
  waiting for transfers between devices  75.3 us (45%)
  blocking collectives  43.6 us (26%)
  between operations  14.9 us (9%)
  starting transfers between devices  10.2 us (6%)
  local copies, waits for them, and re-layouts  9.16 us (5%)
  matrix products  8.18 us (5%)
  other arithmetic  5.46 us (3%)
    psum x1, waiting for transfers between devices, from_root(): return lax.psum(kept, axis)  58 us
    all_gather x1, blocking collectives, on_device(): lax.all_gather(query_token_rows, 'hosts', axis=0, tiled=True)  30.5 us
    unnamed x1, blocking collectives  13.1 us
    all_to_all x1, waiting for transfers between devices, on_device(): lax.all_to_all(accums, 'hosts', split_axis=0, concat_axis=0, tiled=True)  6.74 us
    all_to_all x1, waiting for transfers between devices, on_device(): lax.all_to_all(peaks, 'hosts', split_axis=0, concat_axis=0, tiled=True)  5.63 us
    unnamed x20, local copies, waits for them, and re-layouts  5.27 us
    dot_general x4, matrix products, block_per_head(): jnp.einsum('rgs,sd->rgd', weights.astype(jnp.bfloat16), value_part, prefe...  5.21 us
    all_to_all x1, waiting for transfers between devices, on_device(): lax.all_to_all(totals, 'hosts', split_axis=0, concat_axis=0, tiled=True)  4.86 us
  transfers between devices with their start and end apart: 4, of which 4 were waited for; matrix products, arithmetic and copies ran while one was open for 2% of the time, Pallas kernels for 0%

commit v1 on v0

--- a/solution.py
+++ b/solution.py
@@ -5,6 +5,19 @@
 
 HEAD_SIZE = 128
 MASKED_SCORE = -1e30
+
+
+def ring_gather(value, axis, dim):
+    ways = lax.axis_size(axis)
+    up = [(d, (d + 1) % ways) for d in range(ways)]
+    down = [(d, (d - 1) % ways) for d in range(ways)]
+    earlier, later = ([value], [value])
+    for _ in range(ways // 2):
+        earlier.append(lax.ppermute(earlier[-1], axis, up))
+    for _ in range((ways - 1) // 2):
+        later.append(lax.ppermute(later[-1], axis, down))
+    line = jnp.concatenate([*earlier[::-1], *later[1:]], axis=dim)
+    return jnp.roll(line, (lax.axis_index(axis) - ways // 2) * value.shape[dim], axis=dim)
 
 
 def from_root(value, axis, source):
@@ -108,7 +121,7 @@
     visible = jnp.concatenate([front_visible, own_visible], 1)
     block_out = block_attention(context_queries, key_rows, value_rows, visible, factor)
     all_queries, all_spans = (
-        lax.all_gather(query_token_rows, "hosts", axis=0, tiled=True),
+        ring_gather(query_token_rows, "hosts", 0),
         lax.all_gather(span_start, "hosts", axis=0, tiled=True),
     )
     key_positions = host_index * block_len + positions

time: 168 us -> 148 us (0.88)
  blocking collectives: 43.6 us -> 11.3 us
  starting transfers between devices: 10.2 us -> 25.6 us
  waiting for transfers between devices: 75.3 us -> 69.6 us
  local copies, waits for them, and re-layouts: 9.16 us -> 12.4 us
    all_gather x1 -> x0, blocking collectives: 30.5 us -> none  [on_device(): lax.all_gather(query_token_rows, 'hosts', axis=0, tiled=True)]
    ppermute x0 -> x7, starting transfers between devices: none -> 15.6 us  [the longest x3 12.6 us: ring_gather(): later.append(lax.ppermute(later[-1], axis, down))]
    all_to_all x1, waiting for transfers between devices: 6.74 us -> 0.01 us  [on_device(): lax.all_to_all(accums, 'hosts', split_axis=0, concat_axis=0, tiled=True)]
    ppermute x0 -> x7, waiting for transfers between devices: none -> 3.53 us  [the longest x4 3.52 us: ring_gather(): earlier.append(lax.ppermute(earlier[-1], axis, up))]
    unnamed x1, blocking collectives: 13.1 us -> 11.3 us
    unnamed x20 -> x21, local copies, waits for them, and re-layouts: 5.27 us -> 5.86 us
  transfers between devices with their start and end apart: 4 -> 11, of which waited for: 4 -> 5; matrix products, arithmetic and copies ran while one was open for 2% -> 12% of each run, Pallas kernels for 0% -> 0%
where the time goes in v1:
time: 148 us
  waiting for transfers between devices  69.6 us (47%)
  starting transfers between devices  25.6 us (17%)
  between operations  14.9 us (10%)
  local copies, waits for them, and re-layouts  12.4 us (8%)
  blocking collectives  11.3 us (8%)
  matrix products  8.34 us (6%)
  other arithmetic  5.08 us (3%)
    psum x1, waiting for transfers between devices, from_root(): return lax.psum(kept, axis)  57 us
    ppermute x3, starting transfers between devices, ring_gather(): later.append(lax.ppermute(later[-1], axis, down))  12.6 us
    unnamed x1, blocking collectives  11.3 us
    unnamed x21, local copies, waits for them, and re-layouts  5.86 us
    dot_general x4, matrix products, block_per_head(): jnp.einsum('rgs,sd->rgd', weights.astype(jnp.bfloat16), value_part, prefe...  5.35 us
    all_to_all x1, waiting for transfers between devices, on_device(): lax.all_to_all(peaks, 'hosts', split_axis=0, concat_axis=0, tiled=True)  4.86 us
    all_to_all x1, waiting for transfers between devices, on_device(): lax.all_to_all(totals, 'hosts', split_axis=0, concat_axis=0, tiled=True)  4.23 us
    ppermute x4, waiting for transfers between devices, ring_gather(): earlier.append(lax.ppermute(earlier[-1], axis, up))  3.52 us
  transfers between devices with their start and end apart: 11, of which 5 were waited for; matrix products, arithmetic and copies ran while one was open for 12% of the time, Pallas kernels for 0%

profile of v1, /device:TPU:0, one launch (start us, length us, event | category | flops | bytes accessed | tf_op | source)
XLA Modules:
  0.0 147.5 jit_solution(6282432589137022648)
XLA Ops:
  7.2 3.0 %collective-permute-start = (bf16[1,4096]{1,0:T(2,128)(2,1)}, bf16[1,4096]{1,0:T(2,128)(2,1)S(1)}, u32[]{:S(2)}, u32[]{:S(2)}) collective-permute-start(bf16[1,4096]{1,0:T(2,128)(2,1)} %param.14), channel_id=1, source_target_pairs={{0,2},{2,4},{4,6},{6,8},{8,10},{10,12},{12,14},{14,0},{1,3},{3,5},... | collective-permute-start | bytes 24584 | tf_op jit(solution)/shard_map/ppermute | solution.py:16
  10.2 3.1 %collective-permute-start.4 = (bf16[1,4096]{1,0:T(2,128)(2,1)}, bf16[1,4096]{1,0:T(2,128)(2,1)S(1)}, u32[]{:S(2)}, u32[]{:S(2)}) collective-permute-start(bf16[1,4096]{1,0:T(2,128)(2,1)} %param.14), channel_id=1, source_target_pairs={{0,14},{2,0},{4,2},{6,4},{8,6},{10,8},{12,10},{14,12},{1,15},{3,1}... | collective-permute-start | bytes 24584 | tf_op jit(solution)/shard_map/ppermute | solution.py:18
  13.3 1.9 %collective-permute-done = bf16[1,4096]{1,0:T(2,128)(2,1)S(1)} collective-permute-done((bf16[1,4096]{1,0:T(2,128)(2,1)}, bf16[1,4096]{1,0:T(2,128)(2,1)S(1)}, u32[]{:S(2)}, u32[]{:S(2)}) %collective-permute-start) | collective-permute-done | bytes 8224 | tf_op jit(solution)/shard_map/ppermute | solution.py:16
  15.1 4.8 %collective-permute-start.5 = (bf16[1,4096]{1,0:T(2,128)(2,1)S(1)}, bf16[1,4096]{1,0:T(2,128)(2,1)S(1)}, u32[]{:S(2)}, u32[]{:S(2)}) collective-permute-start(bf16[1,4096]{1,0:T(2,128)(2,1)S(1)} %collective-permute-done.4), channel_id=1, source_target_pairs={{0,14},{2,0},{4,2},{6,4},{8,6},{10,8},{12,10},{14,12},{1,15},{3,1}... | collective-permute-start | bytes 24584 | tf_op jit(solution)/shard_map/ppermute | solution.py:18
  19.9 1.7 %collective-permute-done.1 = bf16[1,4096]{1,0:T(2,128)(2,1)S(1)} collective-permute-done((bf16[1,4096]{1,0:T(2,128)(2,1)S(1)}, bf16[1,4096]{1,0:T(2,128)(2,1)S(1)}, u32[]{:S(2)}, u32[]{:S(2)}) %collective-permute-start.1) | collective-permute-done | bytes 8224 | tf_op jit(solution)/shard_map/ppermute | solution.py:16
  22.2 0.6 copy-done.6
  22.9 0.6 dynamic-slice
  23.5 0.8 dynamic-update-slice
  24.2 4.7 %collective-permute-start.6 = (bf16[1,4096]{1,0:T(2,128)(2,1)S(1)}, bf16[1,4096]{1,0:T(2,128)(2,1)S(1)}, u32[]{:S(2)}, u32[]{:S(2)}) collective-permute-start(bf16[1,4096]{1,0:T(2,128)(2,1)S(1)} %collective-permute-done.5), channel_id=1, source_target_pairs={{0,14},{2,0},{4,2},{6,4},{8,6},{10,8},{12,10},{14,12},{1,15},{3,1}... | collective-permute-start | bytes 24584 | tf_op jit(solution)/shard_map/ppermute | solution.py:18
  29.0 11.3 %all-reduce.1 = s32[8]{0:T(128)S(1)} all-reduce(s32[8]{0:T(128)S(1)} %dynamic-update-slice), channel_id=1, replica_groups=mesh['groups'=2,'hosts'=8,'tensor'=2] {'hosts'}, use_global_device_ids=true, to_apply=%add.1 | all-reduce | flops 8 | bytes 64
  40.3 1.1 copy.26
  41.5 0.6 copy-done.3
  42.0 0.4 concatenate.32
  42.5 2.7 %while.26 = (s32[]{:T(128)}, f32[4,8,8]{2,1,0:T(8,128)S(1)}, f32[4,8,8]{2,1,0:T(8,128)S(1)}, f32[4,8,8,128]{3,2,1,0:T(8,128)S(1)}, bf16[4,8,8,128]{3,2,0,1:T(8,1...) while((s32[]{:T(128)}, f32[4,8,8]{2,1,0:T(8,128)S(1)}, ...), condition=%wide.region_8.9_spmd.clone, body=%wide.region_5.8_spmd.clone.sunk | while | flops 4268930 | bytes 241033 | solution.py:92
  45.3 0.7 all_to_all.18
  45.9 3.3 %all-to-all-start = ((f32[8,1,32]{2,1,0:T(1,128)}), f32[8,1,32]{2,1,0:T(1,128)S(1)}, u32[]{:S(2)}, u32[]{:S(2)}) async-start(f32[8,1,32]{2,1,0:T(1,128)} %bitcast.22), calls=%async_computation | async-start | bytes 8192 | tf_op jit(solution)/shard_map/all_to_all | solution.py:133
  49.3 0.7 maximum_select_fusion
  50.1 0.7 all_to_all.22
  50.8 4.9 %all-to-all-done = f32[8,1,32]{2,1,0:T(1,128)S(1)} async-done(((f32[8,1,32]{2,1,0:T(1,128)}), f32[8,1,32]{2,1,0:T(1,128)S(1)}, u32[]{:S(2)}, u32[]{:S(2)}) %all-to-all-start) | async-done | bytes 1056 | tf_op jit(solution)/shard_map/all_to_all | solution.py:133
  55.6 3.3 %all-to-all-start.2 = ((f32[8,1,32]{2,1,0:T(1,128)}), f32[8,1,32]{2,1,0:T(1,128)S(1)}, u32[]{:S(2)}, u32[]{:S(2)}) async-start(f32[8,1,32]{2,1,0:T(1,128)} %bitcast.29), calls=%async_computation.2 | async-start | bytes 8192 | tf_op jit(solution)/shard_map/all_to_all | solution.py:134
  59.1 0.7 copy.25
  59.7 0.6 concatenate.25
  60.4 0.7 copy.39
  61.0 4.2 %all-to-all-done.2 = f32[8,1,32]{2,1,0:T(1,128)S(1)} async-done(((f32[8,1,32]{2,1,0:T(1,128)}), f32[8,1,32]{2,1,0:T(1,128)S(1)}, u32[]{:S(2)}, u32[]{:S(2)}) %all-to-all-start.2) | async-done | bytes 1056 | tf_op jit(solution)/shard_map/all_to_all | solution.py:134
  65.3 3.4 %all-to-all-start.1 = ((f32[8,1,4096]{2,1,0:T(1,128)}), f32[8,1,4096]{2,1,0:T(1,128)S(1)}, u32[]{:S(2)}, u32[]{:S(2)}) async-start(f32[8,1,4096]{2,1,0:T(1,128)} %bitcast.26), calls=%async_computation.1 | async-start | bytes 262144 | tf_op jit(solution)/shard_map/all_to_all | solution.py:135
  68.7 57.0 %all-reduce.4.cloned.1.call-done = bf16[2,128,512]{1,2,0:T(8,128)(2,1)} async-done(((bf16[2,128,512]{1,2,0:T(8,128)(2,1)}), bf16[2,128,512]{1,2,0:T(8,128)(2,1)}) %all-reduce.4.cloned.1.call-update) | async-done | bytes 262160 | tf_op jit(solution)/shard_map/psum | solution.py:25
  125.7 1.0 fusion.52
  126.7 0.8 maximum_bitcast_fusion
  127.4 10.2 %while.25 = (s32[]{:T(128)}, bf16[4,128,8,128]{3,1,2,0:T(8,128)(2,1)S(1)}, pred[128,256]{1,0:T(8,128)(4,1)}, bf16[4,128,8,128]{1,3,2,0:T(8,128)(2,1)S(1)}, bf16[...) while((s32[]{:T(128)}, bf16[4,128,8,128]{3,1,2,0:T(8,128)(2,1)S(1)}, ...), condition=%wide.region_4.5_spmd, body=%wide.region_1.4_spmd.sunk | while | flops 136840704 | bytes 5089385 | solution.py:60
  127.4 0.3 convolution_multiply_fusion.3
  127.8 0.4 copy-done.4
  128.2 0.4 fusion.69
  128.6 1.3 fusion.70
  130.0 0.3 convolution_multiply_fusion.3
  130.3 0.4 copy-done.4
  130.7 0.4 fusion.69
  131.2 1.3 fusion.70
  132.5 0.3 convolution_multiply_fusion.3
  132.9 0.4 copy-done.4
  133.3 0.4 fusion.69
  133.7 1.3 fusion.70
  135.1 0.3 convolution_multiply_fusion.3
  135.4 0.4 copy-done.4
  135.8 0.4 fusion.69
  136.3 1.3 fusion.70
  137.6 0.7 copy.33
  138.3 1.4 copy.53
  140.1 0.6 divide_convert_fusion
  (62 shorter events, 3.4 us)
Async XLA Ops:
  7.2 8.0 %collective-permute-start = (bf16[1,4096]{1,0:T(2,128)(2,1)}, bf16[1,4096]{1,0:T(2,128)(2,1)S(1)}, u32[]{:S(2)}, u32[]{:S(2)}) collective-permute-start(bf16[1,4096]{1,0:T(2,128)(2,1)} %param.14), channel_id=1, source_target_pairs={{0,2},{2,4},{4,6},{6,8},{8,10},{10,12},{12,14},{14,0},{1,3},{3,5},... | collective-permute-start | bytes 24584 | tf_op jit(solution)/shard_map/ppermute | solution.py:16
  10.2 5.0 %collective-permute-start.4 = (bf16[1,4096]{1,0:T(2,128)(2,1)}, bf16[1,4096]{1,0:T(2,128)(2,1)S(1)}, u32[]{:S(2)}, u32[]{:S(2)}) collective-permute-start(bf16[1,4096]{1,0:T(2,128)(2,1)} %param.14), channel_id=1, source_target_pairs={{0,14},{2,0},{4,2},{6,4},{8,6},{10,8},{12,10},{14,12},{1,15},{3,1}... | collective-permute-start | bytes 24584 | tf_op jit(solution)/shard_map/ppermute | solution.py:18
  15.1 6.4 %collective-permute-start.1 = (bf16[1,4096]{1,0:T(2,128)(2,1)S(1)}, bf16[1,4096]{1,0:T(2,128)(2,1)S(1)}, u32[]{:S(2)}, u32[]{:S(2)}) collective-permute-start(bf16[1,4096]{1,0:T(2,128)(2,1)S(1)} %collective-permute-done), channel_id=1, source_target_pairs={{0,2},{2,4},{4,6},{6,8},{8,10},{10,12},{12,14},{14,0},{1,3},{3,5},... | collective-permute-start | bytes 24584 | tf_op jit(solution)/shard_map/ppermute | solution.py:16
  15.1 9.1 %collective-permute-start.5 = (bf16[1,4096]{1,0:T(2,128)(2,1)S(1)}, bf16[1,4096]{1,0:T(2,128)(2,1)S(1)}, u32[]{:S(2)}, u32[]{:S(2)}) collective-permute-start(bf16[1,4096]{1,0:T(2,128)(2,1)S(1)} %collective-permute-done.4), channel_id=1, source_target_pairs={{0,14},{2,0},{4,2},{6,4},{8,6},{10,8},{12,10},{14,12},{1,15},{3,1}... | collective-permute-start | bytes 24584 | tf_op jit(solution)/shard_map/ppermute | solution.py:18
  21.6 7.4 %collective-permute-start.2 = (bf16[1,4096]{1,0:T(2,128)(2,1)S(1)}, bf16[1,4096]{1,0:T(2,128)(2,1)S(1)}, u32[]{:S(2)}, u32[]{:S(2)}) collective-permute-start(bf16[1,4096]{1,0:T(2,128)(2,1)S(1)} %collective-permute-done.1), channel_id=1, source_target_pairs={{0,2},{2,4},{4,6},{6,8},{8,10},{10,12},{12,14},{14,0},{1,3},{3,5},... | collective-permute-start | bytes 24584 | tf_op jit(solution)/shard_map/ppermute | solution.py:16
  22.2 0.7 copy-start.6
  24.2 17.3 %collective-permute-start.6 = (bf16[1,4096]{1,0:T(2,128)(2,1)S(1)}, bf16[1,4096]{1,0:T(2,128)(2,1)S(1)}, u32[]{:S(2)}, u32[]{:S(2)}) collective-permute-start(bf16[1,4096]{1,0:T(2,128)(2,1)S(1)} %collective-permute-done.5), channel_id=1, source_target_pairs={{0,14},{2,0},{4,2},{6,4},{8,6},{10,8},{12,10},{14,12},{1,15},{3,1}... | collective-permute-start | bytes 24584 | tf_op jit(solution)/shard_map/ppermute | solution.py:18
  29.0 12.5 %collective-permute-start.3 = (bf16[1,4096]{1,0:T(2,128)(2,1)S(1)}, bf16[1,4096]{1,0:T(2,128)(2,1)S(1)}, u32[]{:S(2)}, u32[]{:S(2)}) collective-permute-start(bf16[1,4096]{1,0:T(2,128)(2,1)S(1)} %collective-permute-done.2), channel_id=1, source_target_pairs={{0,2},{2,4},{4,6},{6,8},{8,10},{10,12},{12,14},{14,0},{1,3},{3,5},... | collective-permute-start | bytes 24584 | tf_op jit(solution)/shard_map/ppermute | solution.py:16
  40.3 1.1 copy-start.2
  41.3 0.7 copy-start.3
  42.5 16.6 %copy-start = (bf16[128,4096]{1,0:T(8,128)(2,1)S(1)}, bf16[128,4096]{1,0:T(8,128)(2,1)}, u32[]{:S(2)}) copy-start(bf16[128,4096]{1,0:T(8,128)(2,1)} %param.10) | copy-start | bytes 3145732
  45.9 9.7 %all-to-all-start = ((f32[8,1,32]{2,1,0:T(1,128)}), f32[8,1,32]{2,1,0:T(1,128)S(1)}, u32[]{:S(2)}, u32[]{:S(2)}) async-start(f32[8,1,32]{2,1,0:T(1,128)} %bitcast.22), calls=%async_computation | async-start | bytes 8192 | tf_op jit(solution)/shard_map/all_to_all | solution.py:133
  49.3 76.4 %all-reduce.4.cloned.1.call-start = ((), (), s32[]{:S(2)}) async-start(), calls=%async_computation.3 | async-start | bytes 524288 | tf_op jit(solution)/shard_map/psum | solution.py:25
  50.1 8.9 %copy-start.5 = (s32[128]{0:T(128)S(1)}, s32[128]{0:T(128)}, u32[]{:S(2)}) copy-start(s32[128]{0:T(128)} %param.13) | copy-start | bytes 1540
  55.6 9.6 %all-to-all-start.2 = ((f32[8,1,32]{2,1,0:T(1,128)}), f32[8,1,32]{2,1,0:T(1,128)S(1)}, u32[]{:S(2)}, u32[]{:S(2)}) async-start(f32[8,1,32]{2,1,0:T(1,128)} %bitcast.29), calls=%async_computation.2 | async-start | bytes 8192 | tf_op jit(solution)/shard_map/all_to_all | solution.py:134
  60.4 67.1 %copy-start.1 = (bf16[4,128,8,128]{3,1,2,0:T(8,128)(2,1)S(1)}, bf16[4,128,8,128]{3,1,2,0:T(8,128)(2,1)}, u32[]{:S(2)}) copy-start(bf16[4,128,8,128]{3,1,2,0:T(8,128)(2,1)} %custom-call) | copy-start | bytes 3145732
  65.3 74.5 %all-to-all-start.1 = ((f32[8,1,4096]{2,1,0:T(1,128)}), f32[8,1,4096]{2,1,0:T(1,128)S(1)}, u32[]{:S(2)}, u32[]{:S(2)}) async-start(f32[8,1,4096]{2,1,0:T(1,128)} %bitcast.26), calls=%async_computation.1 | async-start | bytes 262144 | tf_op jit(solution)/shard_map/all_to_all | solution.py:135
  127.4 0.8 copy-start.4
  130.0 0.8 copy-start.4
  132.5 0.8 copy-start.4
  135.1 0.8 copy-start.4
Sparse Core Ops, SparseCore 0:
  53.5 72.1 all-reduce.3
